TPU v7x, 256 devices: a whole 4x4x8 slice. The times are simulated.
256 devices in a mesh: chol: 64 (over z, y_lo, x), walk: 4 (over y_hi, core).
Axes of the slice: x: 4, y: 4 (y_hi: 2, y_lo: 2; y = y_hi * 2 + y_lo), z: 8, core: 2. Of those that a mesh axis runs over, the one named last changes fastest.
Arguments:
- chol_full: float32 [768, 160000], P('chol'), may hold values from -0.109375 to 0.109375
- chol_half: bfloat16 [768, 24000], P('chol'), may hold values from -0.001953125 to 0.001953125
- walkers: bfloat16 [96, 24000], P('walk', 'chol'), may hold values from -6 to 6
- inv_intersection: bfloat16 [96, 60, 60], P('walk'), may hold values from -0.75 to 0.75
- fields: float32 [96, 768], P('walk', 'chol'), may hold values from -6 to 6
- log_weight: float32 [96], P('walk'), may hold values from -4 to 4
Outputs:
- new_walkers: bfloat16 [96, 24000], P('walk', 'chol')
- new_log_weight: float32 [96], P('walk')
- hartree: float32 [96], P('walk')
- mixed_energy: float32 [], replicated
All inputs are finite; a program needn't handle non-finite values.
Results may differ from a plain program's by a relative error of at most 0.0034.
Values may be sent and summed in bfloat16 or wider, within the bound.
A program may use at most 128 MiB of HBM per device.

v0:
```python
import jax
import jax.numpy as jnp
from jax import lax
from jax.sharding import PartitionSpec as P

N = 400
NE = 60
ORDER = 3


field_step = 0.1
bias_coef = 2.0
bias_cap = 0.3


def on_device(chol_full, chol_half, walkers, inv_intersection, fields, log_weight):
    count = walkers.shape[0]
    piece = walkers.shape[1]
    whole = lax.all_gather(walkers, "chol", axis=1, tiled=True)
    orbitals = whole.reshape(count, NE, N)
    green = jnp.einsum(
        "wba,wbi->wai", inv_intersection, orbitals, preferred_element_type=jnp.float32
    ).astype(jnp.bfloat16)
    force_bias = lax.dot_general(
        green.reshape(count, NE * N),
        chol_half,
        (((1,), (1,)), ((), ())),
        preferred_element_type=jnp.float32,
    )
    bias_shift = jnp.clip(-bias_coef * force_bias, -bias_cap, bias_cap)
    field = fields - bias_shift
    local_log = jnp.sum(fields * bias_shift - 0.5 * bias_shift * bias_shift, axis=1)
    local_energy = 0.5 * jnp.sum(force_bias * force_bias, axis=1)
    operator = field_step * jnp.dot(
        field, chol_full, precision=lax.Precision.HIGHEST, preferred_element_type=jnp.float32
    )
    operator = operator.reshape(count, N, N)
    offset = lax.axis_index("chol") * piece
    current = orbitals
    total = walkers.astype(jnp.float32)
    for order in range(1, ORDER + 1):
        partial_value = jnp.einsum(
            "waj,wij->wai", current.astype(jnp.float32), operator, precision=lax.Precision.HIGHEST
        )
        partial_value = partial_value.reshape(count, NE * N) / order
        summed = lax.psum(partial_value, "chol")
        total = total + lax.dynamic_slice_in_dim(summed, offset, piece, 1)
        current = summed.astype(jnp.bfloat16).reshape(count, NE, N)
    new_walkers = total.astype(jnp.bfloat16)
    sums_log, sums_energy = lax.psum((local_log, local_energy), "chol")
    new_log_weight = log_weight + sums_log
    weights = jnp.exp(new_log_weight)
    numerator, denominator = lax.psum((jnp.sum(weights * sums_energy), jnp.sum(weights)), "walk")
    mixed_energy = numerator / denominator
    return (new_walkers, new_log_weight, sums_energy, mixed_energy)


def solution(mesh):
    return jax.shard_map(
        on_device,
        mesh=mesh,
        in_specs=(
            P("chol", None),
            P("chol", None),
            P("walk", "chol"),
            P("walk", None, None),
            P("walk", "chol"),
            P("walk"),
        ),
        out_specs=(P("walk", "chol"), P("walk"), P("walk"), P()),
        check_vma=False,
    )
```

profile of v0, /device:TPU:8, one launch (start us, length us, event | category | flops | bytes accessed | tf_op | source)
XLA Modules:
  0.0 2256.3 jit_solution(8105988015011977656)
XLA Ops:
  7.2 0.0 all-gather.3.cloned.1.call-start
  7.2 0.7 all-gather.3.cloned.1.call-update
  7.9 0.0 all-reduce.6.cloned.1.call-start
  8.0 298.4 %all-gather.3.cloned.1.call-done = bf16[64,375,24]{1,2,0:T(8,128)(2,1)} async-done(((bf16[1,375,24]{1,2,0:T(8,128)(2,1)}), bf16[64,375,24]{1,2,0:T(8,128)(2,1)}) %all-gather.3.cloned.1.call-update) | async-done | bytes 1152016 | tf_op jit(solution)/shard_map/all_gather | solution.py:19
  306.4 1.5 copy.13
  307.9 1.3 reshape.39
  309.2 3.3 reshape.32
  312.5 2.8 convolution_convert_fusion
  315.3 3.1 reshape.33
  318.4 0.5 multiply_reduce_fusion
  318.9 17.4 convolution_multiply_fusion
  336.3 36.6 %reshape.34 = f32[24,400,400]{2,1,0:T(8,128)} reshape(f32[24,160000]{1,0:T(8,128)} %convolution_multiply_fusion) | data formatting | bytes 30720000 | tf_op jit(solution)/shard_map/reshape | solution.py:37
  372.9 16.1 convolution_bitcast_fusion
  389.1 4.1 reshape.35
  393.1 0.0 all-reduce.6.cloned.1.call-update
  393.1 0.2 all-reduce.8.cloned.1.call-start
  393.4 602.8 %all-reduce.6.cloned.1.call-done = f32[24,24000]{1,0:T(8,128)} async-done(((f32[24,24000]{1,0:T(8,128)}), f32[24,24000]{1,0:T(8,128)}) %all-reduce.6.cloned.1.call-update) | async-done | bytes 2304016 | tf_op jit(solution)/shard_map/psum | solution.py:46
  996.2 1.8 convert_element_type.20
  997.9 3.3 reshape.36
  1001.2 16.0 convolution_multiply_fusion.2
  1017.3 4.0 div.23
  1021.3 0.3 all-reduce.10.cloned.1.call-start
  1021.6 599.8 %all-reduce.8.cloned.1.call-done = f32[24,24000]{1,0:T(8,128)} async-done(((f32[24,24000]{1,0:T(8,128)}), f32[24,24000]{1,0:T(8,128)}) %all-reduce.8.cloned.1.call-update) | async-done | bytes 2304016 | tf_op jit(solution)/shard_map/psum | solution.py:46
  1621.4 1.8 convert_element_type.21
  1623.2 3.3 reshape.37
  1626.5 16.1 convolution_multiply_fusion.1
  1642.6 4.1 div.26
  1646.7 147.4 %all-reduce = (f32[24]{0:T(128)S(1)}, f32[24]{0:T(128)S(1)}) all-reduce(f32[24]{0:T(128)S(1)} %get-tuple-element.5, f32[24]{0:T(128)S(1)} %broadcast_multiply_fusion), channel_id=1, replica_groups=mesh['chol'=64,'walk'=4] {'chol'}, use_global_device_ids=true, to_apply=%region_4.5 | all-reduce | flops 48 | bytes 384 | tf_op jit(solution)/shard_map/psum | solution.py:50
  1794.1 1.1 exponential_reduce_fusion
  1795.2 8.1 all-reduce.1
  1804.6 442.3 %all-reduce.10.cloned.1.call-done = f32[24,24000]{1,0:T(8,128)} async-done(((f32[24,24000]{1,0:T(8,128)}), f32[24,24000]{1,0:T(8,128)}) %all-reduce.10.cloned.1.call-update) | async-done | bytes 2304016 | tf_op jit(solution)/shard_map/psum | solution.py:46
  2246.9 1.6 add_convert_fusion
  (15 shorter events, 0.1 us)
Async XLA Ops:
  7.2 311.2 %copy-start = (bf16[12,24000]{1,0:T(8,128)(2,1)S(1)}, bf16[12,24000]{1,0:T(8,128)(2,1)}, u32[]{:S(2)}) copy-start(bf16[12,24000]{1,0:T(8,128)(2,1)} %param.7) | copy-start | bytes 1728004
  7.2 299.2 %all-gather.3.cloned.1.call-start = ((), (), s32[]{:S(2)}) async-start(), calls=%async_computation.3 | async-start | bytes 1198080 | tf_op jit(solution)/shard_map/all_gather | solution.py:19
  7.9 988.3 %all-reduce.6.cloned.1.call-start = ((), (), s32[]{:S(2)}) async-start(), calls=%async_computation | async-start | bytes 4620288 | tf_op jit(solution)/shard_map/psum | solution.py:46
  312.5 5.9 copy-start.3
  393.1 1228.3 %all-reduce.8.cloned.1.call-start = ((), (), s32[]{:S(2)}) async-start(), calls=%async_computation.1 | async-start | bytes 4620288 | tf_op jit(solution)/shard_map/psum | solution.py:46
  1021.3 1225.6 %all-reduce.10.cloned.1.call-start = ((), (), s32[]{:S(2)}) async-start(), calls=%async_computation.2 | async-start | bytes 4620288 | tf_op jit(solution)/shard_map/psum | solution.py:46
  1642.6 605.9 %copy-start.1 = (bf16[12,24000]{1,0:T(8,128)(2,1)S(1)}, bf16[12,24000]{1,0:T(8,128)(2,1)}, u32[]{:S(2)}) copy-start(bf16[12,24000]{1,0:T(8,128)(2,1)} %param.7) | copy-start | bytes 1728004
  1646.6 147.5 %copy-start.4 = (f32[24]{0:T(128)S(1)}, f32[24]{0:T(128)}, u32[]{:S(2)}) copy-start(f32[24]{0:T(128)} %param.11) | copy-start | bytes 292
  1646.6 600.2 %copy-start.2 = (bf16[24,375]{1,0:T(8,128)(2,1)S(1)}, bf16[24,375]{1,0:T(8,128)(2,1)}, u32[]{:S(2)}) copy-start(bf16[24,375]{1,0:T(8,128)(2,1)} %param.8) | copy-start | bytes 54004
  1794.1 454.3 %copy-start.5 = (f32[24]{0:T(128)}, f32[24]{0:T(128)S(1)}, u32[]{:S(2)}) copy-start(f32[24]{0:T(128)S(1)} %get-tuple-element.9) | copy-start | bytes 292
Sparse Core Ops, SparseCore 0:
  9.8 296.5 all-gather.2
  393.3 602.8 all-reduce.5
  1021.4 599.9 all-reduce.7
  1646.8 600.0 all-reduce.9
where the time goes:
time: 2260 us
  waiting for transfers between devices  1940 us (86%)
  blocking collectives  155 us (7%)
  matrix products  69 us (3%)
  local copies, waits for them, and re-layouts  64.5 us (3%)
    psum x3, waiting for transfers between devices, on_device(): summed = lax.psum(partial_value, 'chol')  1640 us
    all_gather x1, waiting for transfers between devices, on_device(): whole = lax.all_gather(walkers, 'chol', axis=1, tiled=True)  298 us
    psum x1, blocking collectives, on_device(): sums_log, sums_energy = lax.psum((local_log, local_energy), 'chol')  147 us
    dot_general x3, matrix products, on_device(): jnp.einsum('waj,wij->wai', current.astype(jnp.float32), operator, precisi...  48.3 us
  transfers between devices with their start and end apart: 4, of which 4 were waited for; matrix products, arithmetic and copies ran while one was open for 0% of the time, Pallas kernels for 0%

commit v1 on v0

v1 whole, which is shorter than its diff:
```python
import jax
import jax.numpy as jnp
from jax import lax
from jax.experimental import pallas as pl
from jax.experimental.pallas import tpu as pltpu
from jax.sharding import PartitionSpec as P

N = 400
NE = 60
ORDER = 3
GROUP = 24
SHARDS = 64
VECTORS = 12
PIECE = 375
COLS = 640
BLOCKS = 250
PLANE = 8
DEPTH = 8
SLICE = 24
LANE = 128
EARLY = 28
STRIDE = 27

field_step = 0.1
bias_coef = 2.0
bias_cap = 0.3

f32 = jnp.float32
bf16 = jnp.bfloat16


def first_tile(r):
    return (N * r) // LANE


def wait_bytes(ref, sem):
    pltpu.make_async_copy(ref, ref, sem).wait()


def kernel(
    chol_hbm, half_hbm, walkers_hbm, inv_hbm, fields_hbm, logw_hbm,
    out_ref, newlog_ref, hartree_ref, mixed_ref,
    half_ref, walkers_ref, inv_ref, fields_ref, logw_ref, cin, csend, crecv, psrc, pp,
    tiles3, tiles4, orb, gflat, gsend, grecv, gf, hsend, hrecv, fsend, frecv,
    f1send, f1recv, f2all, opbuf, oprecv, abuf, xbuf, termt, total, nsend, nrecv,
    in_sem, c_send, c_recv, p_send, p_recv, g_send, g_recv, h_send, h_recv, f_send, f_recv,
    f1_send, f1_recv, f2_send, f2_recv, f3_send, f3_recv, o_send, o_recv, n_send, n_recv,
):
    c = lax.axis_index("chol")
    wk = lax.axis_index("walk")
    core = wk % 2
    z = c // PLANE
    p = c % PLANE
    block = wk * SHARDS + c
    mine = 3 * z + p // 2
    owns = jnp.logical_and((p + core) % 2 == 0, p < 6)
    place = pl.multiple_of(wk * GROUP, 8)

    def owner_of(walker, group):
        return PLANE * (walker // 3) + 2 * (walker % 3) + group % 2

    def send(src, dst, s_sem, r_sem, chol, walk):
        pltpu.make_async_remote_copy(
            src_ref=src, dst_ref=dst, send_sem=s_sem, recv_sem=r_sem,
            device_id={"chol": chol, "walk": walk}, device_id_type=pl.DeviceIdType.MESH,
        ).start()

    base = wk * (SHARDS * COLS) - (wk // 3) * 3840
    pairs = (
        (walkers_hbm, walkers_ref),
        (fields_hbm, fields_ref),
        (half_hbm, half_ref),
        (chol_hbm.at[:, pl.ds(pl.multiple_of(base, LANE), SHARDS * COLS)], cin),
        (inv_hbm, inv_ref),
        (logw_hbm, logw_ref),
    )
    copies = [pltpu.make_async_copy(src, dst, in_sem.at[i]) for i, (src, dst) in enumerate(pairs)]
    for copy in copies:
        copy.start()

    barrier = pltpu.get_barrier_semaphore()

    def greet(i, _):
        pl.semaphore_signal(
            barrier, inc=1, device_id={"chol": (c + i) % SHARDS, "walk": wk},
            device_id_type=pl.DeviceIdType.MESH,
        )
        return 0

    lax.fori_loop(1, SHARDS, greet, 0)
    other_core = wk + 1 - 2 * core
    other_half = (wk + 2) % 4
    beside = PLANE * z + (p + 4) % PLANE
    third = (other_core + 2) % 4
    for chol, walk in ((c, other_core), (beside, other_half), (beside, third)):
        pl.semaphore_signal(
            barrier, inc=1, device_id={"chol": chol, "walk": walk}, device_id_type=pl.DeviceIdType.MESH
        )

    copies[0].wait()
    psrc[...] = jnp.concatenate(
        [walkers_ref[...].astype(f32), jnp.zeros((GROUP, 384 - PIECE), f32)], axis=1
    )
    copies[1].wait()
    fields = jnp.concatenate([fields_ref[...], jnp.zeros((4, GROUP), f32)], axis=0).T
    fields = jnp.concatenate([fields, jnp.zeros((GROUP, 112), f32)], axis=1)
    fsend[...] = pltpu.roll(fields, 16 * p, 1)
    frecv[p] = fsend[...]
    pl.semaphore_wait(barrier, SHARDS + 2)

    def send_piece(i, _):
        walker = (i + c) % GROUP
        owner = owner_of(walker, wk)

        @pl.when(owner != c)
        def _():
            send(psrc.at[pl.ds(walker, 1)], pp.at[pl.ds(c, 1)], p_send, p_recv, owner, wk)

        @pl.when(owner == c)
        def _():
            pltpu.make_async_copy(psrc.at[pl.ds(walker, 1)], pp.at[pl.ds(c, 1)], p_recv).start()

        return 0

    lax.fori_loop(0, GROUP, send_piece, 0)

    copies[4].wait()
    copies[5].wait()

    @pl.when(owns)
    def _():
        third = lax.broadcasted_iota(jnp.int32, (NE, GROUP, NE), 1)
        inverse = jnp.sum(jnp.where(third == mine, inv_ref[...].astype(f32), 0.0), axis=1)
        inverse = jnp.concatenate([inverse, jnp.zeros((4, NE), f32)], axis=0)
        inverse = jnp.concatenate([inverse, jnp.zeros((64, 4), f32)], axis=1).T.astype(bf16)
        wait_bytes(pp, p_recv)
        for q in range(3):
            tiles3[q] = pp[:, q * LANE : (q + 1) * LANE]
        for q in range(4):
            tiles4[q] = jnp.zeros((64, LANE), f32)
        rows = [
            jnp.concatenate([tiles3[q, pl.ds(s, 4, stride=16), :] for q in range(3)], axis=1)
            for s in range(16)
        ]
        for b in range(15):
            line = jnp.concatenate(
                [rows[b][:, 25 * b : PIECE], rows[b + 1][:, : 25 * (b + 1)], jnp.zeros((4, 112), f32)],
                axis=1,
            )
            for q in range(4):
                tiles4[q, pl.ds(b, 4, stride=15), :] = line[:, q * LANE : (q + 1) * LANE]
        orbitals = jnp.concatenate([tiles4[q] for q in range(4)], axis=1)
        green = jnp.dot(inverse, orbitals.astype(bf16), preferred_element_type=f32)
        for q in range(4):
            tiles4[q] = green[:, q * LANE : (q + 1) * LANE]
        flat = [jnp.zeros((8, LANE), f32) for _ in range(25)]
        for r in range(8):
            line = jnp.concatenate([tiles4[q, pl.ds(r, 8, stride=8), :] for q in range(4)], axis=1)
            if r:
                line = pltpu.roll(line, 16 * r, 1)
            for q in range(4):
                flat[first_tile(r) + q] = flat[first_tile(r) + q] + line[:, q * LANE : (q + 1) * LANE]
        for t in range(25):
            gflat[pl.ds(t, 8, stride=25), :] = flat[t]
        for q in range(PLANE):
            part = gflat[SLICE * q : SLICE * (q + 1), :]
            gsend[q] = jnp.concatenate([part, jnp.zeros((8, LANE), f32)], axis=0).astype(bf16)
        grecv[mine] = gsend[p]

        def spread(k, _):
            d = (c + STRIDE * k) % SHARDS
            send(gsend.at[d % PLANE], grecv.at[mine], g_send, g_recv.at[z], d, wk)
            return 0

        lax.fori_loop(1, SHARDS, spread, 0)
        orb[...] = orbitals

    copies[2].wait()
    for q in range(PLANE):
        width = min(SLICE * LANE, NE * N - q * SLICE * LANE)
        part = half_ref[:, q * SLICE * LANE : q * SLICE * LANE + width].astype(f32)
        if width < SLICE * LANE:
            part = jnp.concatenate([part, jnp.zeros((VECTORS, SLICE * LANE - width), f32)], axis=1)
        part = jnp.concatenate([part, jnp.zeros((4, SLICE * LANE), f32)], axis=0)
        hsend[q] = part.astype(bf16)
    row = pl.multiple_of(p * 16, 16)
    hrecv[pl.ds(row, 16), :] = hsend[p]

    def to_plane(k, _):
        q = (p + k) % PLANE
        send(hsend.at[q], hrecv.at[pl.ds(row, 16)], h_send, h_recv, PLANE * z + q, wk)
        send(fsend, frecv.at[p], f_send, f_recv, PLANE * z + q, wk)
        return 0

    lax.fori_loop(1, PLANE, to_plane, 0)

    def cut(d):
        at = (wk // 3) * 3840 + d * COLS - (wk // 3) * (d // 58) * (d - 57) * COLS
        part = cin[:, pl.ds(pl.multiple_of(at, LANE), COLS)]
        last = part[:, 512:]
        under = jnp.concatenate([last[0:4], last[4:8], last[8:12], jnp.zeros((4, LANE), f32)], axis=1)
        return jnp.concatenate([part[:, :512], under], axis=0).astype(bf16)

    slot = pl.multiple_of(c * 16, 16)

    def send_columns(i, _):
        d = (c + STRIDE * i) % SHARDS
        csend[d] = cut(d)
        send(csend.at[d], crecv.at[pl.ds(slot, 16)], c_send, c_recv, d, wk)
        return 0

    copies[3].wait()
    lax.fori_loop(1, EARLY, send_columns, 0)
    @pl.when(owns)
    def _():
        wait_bytes(grecv.at[pl.ds(0, 2)], g_recv.at[z])

    @pl.when(jnp.logical_not(owns))
    def _():
        wait_bytes(grecv.at[pl.ds(0, 3)], g_recv.at[z])

    lax.fori_loop(EARLY, SHARDS, send_columns, 0)
    crecv[pl.ds(slot, 16), :] = cut(c)

    def rest(k, _):
        wait_bytes(grecv.at[pl.ds(0, 3)], g_recv.at[(z + k) % DEPTH])
        return 0

    lax.fori_loop(1, DEPTH, rest, 0)

    for w in range(GROUP):
        gf[32 * w : 32 * w + 32, :] = grecv[w].astype(f32)
    green = jnp.concatenate(
        [gf[pl.ds(t, GROUP, stride=32), :] for t in range(SLICE)], axis=1
    ).astype(bf16)
    wait_bytes(gf.at[pl.ds(0, 7 * GROUP)], f_recv)
    wait_bytes(hrecv.at[pl.ds(0, 7 * 16)], h_recv)
    f1send[...] = lax.dot_general(
        green, hrecv[...], (((1,), (1,)), ((), ())), preferred_element_type=f32
    )
    f1recv[p] = f1send[...]

    def partial_bias(k, _):
        send(f1send, f1recv.at[p], f1_send, f1_recv, PLANE * z + (p + k) % PLANE, wk)
        return 0

    lax.fori_loop(1, PLANE, partial_bias, 0)
    wait_bytes(gf.at[pl.ds(0, 7 * GROUP)], f1_recv)
    force_bias = f1recv[0]
    fields = frecv[0]
    for q in range(1, PLANE):
        force_bias = force_bias + f1recv[q]
        fields = fields + frecv[q]
    shift = jnp.clip(-bias_coef * force_bias, -bias_cap, bias_cap)
    plane_log = jnp.sum(fields * shift - 0.5 * shift * shift, axis=1, keepdims=True)
    plane_energy = 0.5 * jnp.sum(force_bias * force_bias, axis=1, keepdims=True)
    eye = (
        lax.broadcasted_iota(jnp.int32, (GROUP, GROUP), 0)
        == lax.broadcasted_iota(jnp.int32, (GROUP, GROUP), 1)
    )
    log_column = jnp.sum(jnp.where(eye, logw_ref[...], 0.0), axis=1, keepdims=True)
    lane = lax.broadcasted_iota(jnp.int32, (GROUP, LANE), 1)
    wide = fields - shift
    wide = jnp.where(lane == 12, plane_log, wide)
    wide = jnp.where(lane == 13, plane_energy, wide)
    wide = jnp.where(lane == 14, log_column, wide)

    f2all[z, pl.ds(place, GROUP), :] = wide
    planes = f2all.at[z, pl.ds(place, GROUP)]

    def fields_z(k, _):
        send(planes, planes, f2_send, f2_recv, c + PLANE * ((z + k) % DEPTH - z), wk)
        return 0

    lax.fori_loop(1, DEPTH, fields_z, 0)
    wait_bytes(gf.at[pl.ds(0, 7 * GROUP)], f2_recv)
    own = f2all.at[:, pl.ds(place, GROUP)]

    def part(group, k):
        return f2all.at[k, pl.ds(pl.multiple_of(group * GROUP, 8), GROUP)]

    def to_half(k, _):
        send(part(wk, k), part(wk, k), f3_send.at[0], f3_recv.at[0], beside, other_half)
        return 0

    def to_core(k, _):
        send(part(wk, k), part(wk, k), f3_send.at[1], f3_recv.at[1], c, other_core)
        return 0

    def to_third(k, _):
        send(part(wk, k), part(wk, k), f3_send.at[2], f3_recv.at[2], beside, third)
        return 0

    lax.fori_loop(0, DEPTH, to_core, 0)
    lax.fori_loop(0, DEPTH, to_half, 0)
    lax.fori_loop(0, DEPTH, to_third, 0)
    wait_bytes(own, f3_recv.at[1])

    wait_bytes(crecv.at[pl.ds(0, 63 * 16)], c_recv)
    lane96 = lax.broadcasted_iota(jnp.int32, (96, LANE), 1)
    under48 = lane96[:48] % 16 >= 12

    def both(x):
        high = x.astype(bf16)
        return jnp.concatenate([high, (x - high.astype(f32)).astype(bf16)], axis=0)

    def blocks(pair):
        at = pl.multiple_of(48 * pair, 16)

        def block_step(b, acc):
            field = f2all[b, pl.ds(at, 48), :]
            rows = crecv[pl.ds(pl.multiple_of(b * LANE, LANE), LANE), :]
            upper = jnp.dot(both(jnp.where(under48, 0.0, field)), rows, preferred_element_type=f32)
            last = acc[1]
            for q in range(3):
                turned = jnp.where(under48, pltpu.roll(field, 12 - 4 * q, 1), 0.0)
                last = last + jnp.dot(
                    both(turned), rows[:, q * LANE : (q + 1) * LANE], preferred_element_type=f32
                )
            return acc[0] + upper, last

        acc, last = lax.fori_loop(
            0, DEPTH, block_step, (jnp.zeros((96, 512), f32), jnp.zeros((96, LANE), f32))
        )
        for t in range(5):
            part = acc[:, t * LANE : (t + 1) * LANE] if t < 4 else last
            opbuf[pl.ds(8 * at + t, 48, stride=8), :] = field_step * (part[:48] + part[48:])

        def send_block(i, _):
            w = at + (19 * i + block) % 48
            group = w // GROUP
            owner = owner_of(w % GROUP, group)
            me = jnp.logical_and(owner == c, group == wk)
            src = opbuf.at[pl.ds(pl.multiple_of(8 * w, 8), 5)]
            dst = oprecv.at[pl.ds(5 * block, 5)]

            @pl.when(jnp.logical_not(me))
            def _():
                send(src, dst, o_send, o_recv, owner, group)

            @pl.when(me)
            def _():
                pltpu.make_async_copy(src, dst, o_recv).start()

            return 0

        @pl.when(block < BLOCKS)
        def _():
            lax.fori_loop(0, 48, send_block, 0)

    blocks(wk // 2)
    wait_bytes(own, f3_recv.at[0])
    wait_bytes(own, f3_recv.at[2])
    blocks(1 - wk // 2)

    sums = f2all[0]
    for b in range(1, DEPTH):
        sums = sums + f2all[b]
    increment = jnp.sum(jnp.where(lane96 == 12, sums, 0.0), axis=1, keepdims=True)
    energy = jnp.sum(jnp.where(lane96 == 13, sums, 0.0), axis=1, keepdims=True)
    logs = jnp.sum(jnp.where(lane96 == 14, f2all[0], 0.0), axis=1, keepdims=True) + increment
    weight = jnp.exp(logs)
    mixed_ref[...] = jnp.sum(weight * energy, axis=0, keepdims=True) / jnp.sum(weight, axis=0, keepdims=True)
    own_log = jnp.zeros((GROUP, 1), f32)
    own_energy = jnp.zeros((GROUP, 1), f32)
    for g in range(4):
        own_log = jnp.where(wk == g, logs[g * GROUP : (g + 1) * GROUP], own_log)
        own_energy = jnp.where(wk == g, energy[g * GROUP : (g + 1) * GROUP], own_energy)
    newlog_ref[...] = jnp.sum(jnp.where(eye, own_log, 0.0), axis=0, keepdims=True)
    hartree_ref[...] = jnp.sum(jnp.where(eye, own_energy, 0.0), axis=0, keepdims=True)

    @pl.when(owns)
    def _():
        start = jnp.concatenate([orb[...].T[:N], jnp.zeros((N, 64), f32)], axis=1)
        total[...] = start
        xbuf[0:112, :] = jnp.zeros((112, LANE), bf16)
        xbuf[512:624, :] = jnp.zeros((112, LANE), bf16)
        xbuf[112:512, :] = start.astype(bf16)
        wait_bytes(oprecv, o_recv)
        for t in range(25):
            abuf[0:50, t * LANE : (t + 1) * LANE] = oprecv[pl.ds(t, 50, stride=25), :].astype(bf16)
        for k in range(1, ORDER + 1):
            for r in range(8):
                at = first_tile(r) * LANE
                value = jnp.dot(
                    abuf[0:50, at : at + 512], xbuf[112 - 16 * r : 624 - 16 * r, :],
                    preferred_element_type=f32,
                )
                termt[pl.ds(r, 50, stride=8), :] = value / k
            term = termt[...]
            total[...] += term
            if k < ORDER:
                xbuf[112:512, :] = term.astype(bf16)
        new = total[...].astype(bf16).astype(f32).T[:64]
        new = jnp.concatenate([new, jnp.zeros((64, 112), f32)], axis=1)
        for q in range(4):
            tiles4[q] = new[:, q * LANE : (q + 1) * LANE]
        rows = [
            jnp.concatenate([tiles4[q, pl.ds(b, 4, stride=15), :] for q in range(4)], axis=1)
            for b in range(15)
        ]
        for s in range(16):
            parts = []
            if s > 0:
                parts.append(rows[s - 1][:, N - 25 * s : N])
            if s < 15:
                parts.append(rows[s][:, : PIECE - 25 * s])
            piece = jnp.concatenate(parts + [jnp.zeros((4, 384 - PIECE), f32)], axis=1)
            for q in range(3):
                tiles3[q, pl.ds(s, 4, stride=16), :] = piece[:, q * LANE : (q + 1) * LANE]
        for q in range(3):
            nsend[:, q * LANE : (q + 1) * LANE] = tiles3[q]
        pltpu.make_async_copy(nsend.at[pl.ds(c, 1)], nrecv.at[pl.ds(mine, 1)], n_recv).start()

        def scatter(k, _):
            to = (c + STRIDE * k) % SHARDS
            send(nsend.at[pl.ds(to, 1)], nrecv.at[pl.ds(mine, 1)], n_send, n_recv, to, wk)
            return 0

        lax.fori_loop(1, SHARDS, scatter, 0)

    wait_bytes(nrecv, n_recv)
    out_ref[...] = nrecv[:, :PIECE].astype(bf16)

    wait_bytes(crecv.at[pl.ds(0, 63 * 16)], c_send)
    wait_bytes(hrecv.at[pl.ds(0, 7 * 16)], h_send)
    wait_bytes(gf.at[pl.ds(0, 7 * GROUP)], f_send)
    wait_bytes(gf.at[pl.ds(0, 7 * GROUP)], f1_send)
    wait_bytes(gf.at[pl.ds(0, 7 * GROUP)], f2_send)
    for k in range(3):
        wait_bytes(own, f3_send.at[k])

    @pl.when(owns)
    def _():
        wait_bytes(gf.at[pl.ds(0, 23 * 3)], p_send)
        wait_bytes(gf.at[pl.ds(0, 63 * 16)], g_send)
        wait_bytes(gf.at[pl.ds(0, 63 * 3)], n_send)

    @pl.when(jnp.logical_not(owns))
    def _():
        wait_bytes(gf.at[pl.ds(0, 24 * 3)], p_send)

    @pl.when(jnp.logical_and(block < BLOCKS, owns))
    def _():
        wait_bytes(opbuf.at[pl.ds(0, 475)], o_send)

    @pl.when(jnp.logical_and(block < BLOCKS, jnp.logical_not(owns)))
    def _():
        wait_bytes(opbuf.at[pl.ds(0, 480)], o_send)


def on_device(chol_full, chol_half, walkers, inv_intersection, fields, log_weight):
    vmem = pl.BlockSpec(memory_space=pltpu.VMEM)
    dma = pltpu.SemaphoreType.DMA
    new_walkers, new_log, hartree, mixed = pl.pallas_call(
        kernel,
        out_shape=(
            jax.ShapeDtypeStruct((GROUP, PIECE), bf16),
            jax.ShapeDtypeStruct((1, GROUP), f32),
            jax.ShapeDtypeStruct((1, GROUP), f32),
            jax.ShapeDtypeStruct((1, 1), f32),
        ),
        in_specs=[pl.BlockSpec(memory_space=pltpu.HBM)] * 6,
        out_specs=(vmem,) * 4,
        scratch_shapes=[
            pltpu.VMEM((VECTORS, NE * N), bf16),
            pltpu.VMEM((GROUP, PIECE), bf16),
            pltpu.VMEM((NE, GROUP, NE), bf16),
            pltpu.VMEM((VECTORS, GROUP), f32),
            pltpu.VMEM((1, GROUP), f32),
            pltpu.VMEM((VECTORS, SHARDS * COLS), f32),
            pltpu.VMEM((SHARDS, 16, 512), bf16),
            pltpu.VMEM((SHARDS * 16, 512), bf16),
            pltpu.VMEM((GROUP, 384), f32),
            pltpu.VMEM((SHARDS, 384), f32),
            pltpu.VMEM((3, 64, LANE), f32),
            pltpu.VMEM((4, 64, LANE), f32),
            pltpu.VMEM((64, 512), f32),
            pltpu.VMEM((200, LANE), f32),
            pltpu.VMEM((PLANE, 32, LANE), bf16),
            pltpu.VMEM((GROUP, 32, LANE), bf16),
            pltpu.VMEM((1024, LANE), f32),
            pltpu.VMEM((PLANE, 16, SLICE * LANE), bf16),
            pltpu.VMEM((PLANE * 16, SLICE * LANE), bf16),
            pltpu.VMEM((GROUP, LANE), f32),
            pltpu.VMEM((PLANE, GROUP, LANE), f32),
            pltpu.VMEM((GROUP, LANE), f32),
            pltpu.VMEM((PLANE, GROUP, LANE), f32),
            pltpu.VMEM((DEPTH, 96, LANE), f32),
            pltpu.VMEM((96 * 8, LANE), f32),
            pltpu.VMEM((BLOCKS * 5, LANE), f32),
            pltpu.VMEM((64, 25 * LANE), bf16),
            pltpu.VMEM((624, LANE), bf16),
            pltpu.VMEM((N, LANE), f32),
            pltpu.VMEM((N, LANE), f32),
            pltpu.VMEM((SHARDS, 384), f32),
            pltpu.VMEM((GROUP, 384), f32),
            dma((6,)),
        ] + [dma] * 5 + [dma((DEPTH,))] + [dma] * 8 + [dma((3,)), dma((3,))] + [dma] * 4,
        compiler_params=pltpu.CompilerParams(
            has_side_effects=True, collective_id=0, vmem_limit_bytes=60 * 1024 * 1024
        ),
        name="propagate",
    )(
        chol_full, chol_half, walkers, inv_intersection.transpose(1, 0, 2), fields.T,
        log_weight.reshape(1, GROUP),
    )
    return new_walkers, new_log.reshape(GROUP), hartree.reshape(GROUP), mixed.reshape(())


def solution(mesh):
    return jax.shard_map(
        on_device,
        mesh=mesh,
        in_specs=(
            P("chol", None),
            P("chol", None),
            P("walk", "chol"),
            P("walk", None, None),
            P("walk", "chol"),
            P("walk"),
        ),
        out_specs=(P("walk", "chol"), P("walk"), P("walk"), P()),
        check_vma=False,
    )
```

time: 2260 us -> 81.6 us (0.04)
  waiting for transfers between devices: 1940 us -> 0 us
  blocking collectives: 155 us -> 0 us
  Pallas kernels: 0 us -> 75.4 us
  matrix products: 69 us -> 0 us
  local copies, waits for them, and re-layouts: 64.5 us -> 3.65 us
    psum x3 -> x0, waiting for transfers between devices: 1640 us -> none  [on_device(): summed = lax.psum(partial_value, 'chol')]
    all_gather x1 -> x0, waiting for transfers between devices: 298 us -> none  [on_device(): whole = lax.all_gather(walkers, 'chol', axis=1, tiled=True)]
    psum x2 -> x0, blocking collectives: 155 us -> none  [the longest x1 147 us: on_device(): sums_log, sums_energy = lax.psum((local_log, local_energy), 'chol')]
    pallas_call x0 -> x1, Pallas kernels: none -> 75.4 us  [on_device(): pl.pallas_call(kernel, out_shape=(jax.ShapeDtypeStruct((GROUP, PIECE), bf...]
    dot_general x6 -> x0, matrix products: 69 us -> none  [the longest x3 48.3 us: on_device(): jnp.einsum('waj,wij->wai', current.astype(jnp.float32), operator, precisi...]
    reshape x6 -> x0, local copies, waits for them, and re-layouts: 53.6 us -> none  [the longest x1 36.6 us: on_device(): operator = operator.reshape(count, N, N)]
  transfers between devices with their start and end apart: 4 -> 0, of which waited for: 4 -> 0; matrix products, arithmetic and copies ran while one was open for 0% -> 0% of each run, Pallas kernels for 0% -> 0%
where the time goes in v1:
time: 81.6 us; the launch traced here: 81.4 us
  Pallas kernels  75.4 us (92%)
  local copies, waits for them, and re-layouts  3.65 us (4%)
  between operations  2.39 us (3%)
    pallas_call x1, Pallas kernels, on_device(): pl.pallas_call(kernel, out_shape=(jax.ShapeDtypeStruct((GROUP, PIECE), bf...  75.4 us
    unnamed x3, local copies, waits for them, and re-layouts  3.65 us

profile of v1, /device:TPU:8, one launch (start us, length us, event | category | flops | bytes accessed | tf_op | source)
XLA Modules:
  0.0 81.4 jit_solution(15161533239672751418)
XLA Ops:
  0.6 75.4 %propagate.1 = (bf16[24,375]{1,0:T(8,128)(2,1)}, f32[1,24]{1,0:T(1,128)}, f32[1,24]{1,0:T(1,128)}, f32[1,1]{1,0:T(1,128)}) custom-call(f32[12,160000]{1,0:T(8,128)} %chol_hbm.1, bf16[12,24000]{1,0:T(8,128)(2,1)} %half_hbm.1, bf16[24,375]{1,0:T(8,128)(2,1)} %walkers_hbm.1, bf16[60,24,60]{2,1,0:T(8,128)(2,1)} %bitcast.6, f32[12,24]{1,0:T(8,128)} %bitcast.7, ...), custom_call_target="tpu_custom_call" | custom-call | tf_op jit(solution)/shard_map/propagate/pallas_call | solution.py:455
  76.0 1.3 %copy.14 = bf16[24,375]{1,0:T(8,128)(2,1)} copy(bf16[24,375]{1,0:T(8,128)(2,1)} %get-tuple-element.16) | data formatting | bytes 36000
  77.4 1.2 %copy.15 = f32[24]{0:T(128)} copy(f32[24]{0:T(128)} %bitcast.10) | data formatting | bytes 192
  78.6 1.1 %copy.16 = f32[24]{0:T(128)} copy(f32[24]{0:T(128)} %bitcast.9) | data formatting | bytes 192
